TPU v7x, 512 devices: a whole 4x8x8 slice. The times are simulated.
512 devices in a mesh: row: 64 (over z, x, core), grp: 8 (over y).
Axes of the slice: x: 4, y: 8, z: 8, core: 2. Of those that a mesh axis runs over, the one named last changes fastest.
Arguments:
- panel_rows: bfloat16 [262144, 1024], P(('row', 'grp')), may hold values from -300 to 300, as said below
- sign_bits: int32 [262144], P(('row', 'grp')), may hold values from 0 to 1
- sample_rows: int32 [8192], replicated, may hold values from 0 to 262143, as said below
Outputs:
- factor: float32 [1024, 1024], P('row', 'grp')
Inputs may be any that keep to these rules, and one draw needn't show every extreme that they name: `sample_rows`: distinct and ascending. Each aligned block of 512 rows (the rows of one device) holds at most 32 sampled rows, and at least a quarter of these blocks hold exactly 32. `panel_rows`: finite values.
All inputs are finite; a program needn't handle non-finite values.
Results may differ from a plain program's by a relative error of at most 0.0011.
Values may be sent and summed in bfloat16 or wider, within the bound.
A program may use at most 64 MiB of HBM per device.

v0:
```python
import math

import jax
import jax.numpy as jnp
from jax import lax
from jax.sharding import PartitionSpec as P


def hadamard(table_size, dtype):
    row_ids = lax.broadcasted_iota(jnp.int32, (table_size, table_size), 0)
    col_ids = lax.broadcasted_iota(jnp.int32, (table_size, table_size), 1)
    shared = row_ids & col_ids
    parity = jnp.zeros((table_size, table_size), jnp.int32)
    for bit_pos in range(table_size.bit_length() - 1):
        parity = parity ^ shared >> bit_pos & 1
    return (1 - 2 * parity).astype(dtype)


def mix_lead(exchanged):
    lead_table = hadamard(exchanged.shape[0], jnp.float32)
    return jnp.einsum("ab,bic->aic", lead_table, exchanged, precision=lax.Precision.HIGHEST)


def mix_grp(exchanged):
    return lax.all_to_all(mix_lead(exchanged), "grp", split_axis=0, concat_axis=2, tiled=True)


def mix_row(exchanged):
    return lax.all_to_all(mix_lead(exchanged), "row", split_axis=0, concat_axis=1, tiled=True)


def local(panel_rows, sign_bits, sample_rows):
    rows_dev, n_cols = panel_rows.shape
    n_row = lax.axis_size("row")
    n_grp = lax.axis_size("grp")
    flipped = panel_rows * (1 - 2 * sign_bits).astype(jnp.bfloat16)[:, None]
    local_table = hadamard(rows_dev, jnp.bfloat16)
    local_mix = jnp.dot(local_table, flipped, preferred_element_type=jnp.float32)
    grp_mixed = mix_grp(
        lax.all_to_all(local_mix[None], "grp", split_axis=2, concat_axis=0, tiled=True)
    )
    num_samples = sample_rows.shape[0]
    total_rows = rows_dev * n_row * n_grp
    norm_scale = 1.0 / math.sqrt(total_rows * num_samples)
    col_width = n_cols // n_grp
    col_start = lax.axis_index("grp") * col_width
    full_mix = mix_row(lax.all_to_all(grp_mixed, "row", split_axis=1, concat_axis=0, tiled=True))[0]
    capacity = 2 * num_samples // (n_row * n_grp)
    device_id = lax.axis_index("row") * n_grp + lax.axis_index("grp")
    base_row = device_id * rows_dev
    first_slot = jnp.sum((sample_rows < base_row).astype(jnp.int32))
    padded_ids = jnp.concatenate([sample_rows, jnp.full((capacity,), total_rows, jnp.int32)])
    window = lax.dynamic_slice_in_dim(padded_ids, first_slot, capacity)
    local_ids = window - base_row
    is_valid = local_ids < rows_dev
    picked = jnp.take(full_mix, jnp.clip(local_ids, 0, rows_dev - 1), axis=0)
    sketch = jnp.where(is_valid[:, None], picked * norm_scale, 0.0).astype(jnp.bfloat16)
    shard_rows = lax.all_gather(sketch, "grp", axis=0, tiled=True)
    own_cols = lax.dynamic_slice_in_dim(shard_rows, col_start, col_width, 1)
    partial_value = lax.dot_general(
        shard_rows, own_cols, (((0,), (0,)), ((), ())), preferred_element_type=jnp.float32
    )
    gram_block = lax.psum_scatter(partial_value, "row", scatter_dimension=0, tiled=True)
    gathered = lax.all_gather(gram_block[None], ("row", "grp"), axis=0, tiled=True)
    gram_matrix = (
        gathered.reshape(n_row, n_grp, n_cols // n_row, col_width)
        .transpose(0, 2, 1, 3)
        .reshape(n_cols, n_cols)
    )
    lower_factor = jnp.linalg.cholesky(gram_matrix)
    row_width = n_cols // n_row
    return lax.dynamic_slice(
        lower_factor, (lax.axis_index("row") * row_width, col_start), (row_width, col_width)
    )


def solution(mesh):
    return jax.shard_map(
        local,
        mesh=mesh,
        in_specs=(P(("row", "grp"), None), P(("row", "grp")), P()),
        out_specs=P("row", "grp"),
        check_vma=False,
    )
```

profile of v0, /device:TPU:1, one launch (start us, length us, event | category | flops | bytes accessed | tf_op | source)
XLA Modules:
  0.0 839.8 jit_solution(3151985562757183908)
XLA Ops:
  16.0 55.9 %all_to_all.57 = f32[1,512,1024]{1,0,2:T(1,128)S(1)} all-to-all(f32[1,512,1024]{1,0,2:T(1,128)S(1)} %copy.17), channel_id=1, replica_groups=mesh['row'=64,'grp'=8] {'grp'}, dimensions={2} | all-to-all | bytes 4194304 | tf_op jit(solution)/shard_map/all_to_all | solution.py:40
  77.8 51.2 %all_to_all.58 = f32[8,512,128]{2,1,0:T(8,128)S(1)} all-to-all(f32[8,512,128]{2,1,0:T(8,128)S(1)} %copy.19), channel_id=1, replica_groups=mesh['row'=64,'grp'=8] {'grp'}, dimensions={0} | all-to-all | bytes 4194304 | tf_op jit(solution)/shard_map/all_to_all | solution.py:25
  135.6 67.5 %all_to_all.59 = f32[1,512,1024]{2,0,1:T(1,128)S(1)} all-to-all(f32[1,512,1024]{2,0,1:T(1,128)S(1)} %copy.21), channel_id=1, replica_groups=mesh['row'=64,'grp'=8] {'row'}, dimensions={1} | all-to-all | bytes 4194304 | tf_op jit(solution)/shard_map/all_to_all | solution.py:47
  209.2 7.0 all-to-all-start.3
  219.0 46.9 %all-to-all-done.3 = f32[64,8,1024]{2,1,0:T(8,128)S(1)} async-done(((f32[64,8,1024]{2,1,0:T(8,128)}), f32[64,8,1024]{2,1,0:T(8,128)S(1)}, u32[]{:S(2)}, u32[]{:S(2)}) %all-to-all-start.3) | async-done | bytes 2097184 | tf_op jit(solution)/shard_map/all_to_all | solution.py:29
  266.6 19.9 %all_gather.6 = bf16[256,1024]{1,0:T(8,128)(2,1)S(1)} all-gather(bf16[32,1024]{1,0:T(8,128)(2,1)S(1)} %select_convert_fusion), channel_id=1, replica_groups=mesh['row'=64,'grp'=8] {'grp'}, dimensions={0}, use_global_device_ids=true | all-gather | bytes 589824 | tf_op jit(solution)/shard_map/all_gather | solution.py:58
  289.6 188.7 %all-reduce.5.cloned.1.call-done = f32[1024,128]{1,0:T(8,128)} async-done(((f32[1024,128]{1,0:T(8,128)}), f32[1024,128]{1,0:T(8,128)}) %all-reduce.5.cloned.1.call-update) | async-done | bytes 524304
  479.6 120.7 %all-gather.3.cloned.1.call-done = f32[8192,128]{1,0:T(8,128)} async-done(((f32[16,128]{1,0:T(8,128)}), f32[8192,128]{1,0:T(8,128)}) %all-gather.3.cloned.1.call-update) | async-done | bytes 4194320 | tf_op jit(solution)/shard_map/all_gather | solution.py:64
  607.8 5.3 copy.25
  620.1 11.7 %cholesky.223 = f32[128,128]{1,0:T(8,128)S(1)} custom-call(f32[128,128]{1,0:T(8,128)S(1)} %cholesky.580), custom_call_target="Cholesky" | custom-call | tf_op jit(solution)/shard_map/jit(cholesky)/cholesky | solution.py:70
  631.8 9.8 %custom-call.59 = f32[1,128,128]{1,2,0:T(8,128)S(1)} custom-call(f32[1,128,128]{2,1,0:T(8,128)S(1)} %get-tuple-element.30), custom_call_target="InvertDiagBlocksLowerTriangular" | custom-call | tf_op jit(solution)/shard_map/jit(cholesky)/cholesky | solution.py:70
  648.1 20.4 %cholesky.244 = f32[128,128]{1,0:T(8,128)S(1)} custom-call(f32[128,128]{1,0:T(8,128)S(1)} %cholesky.584), custom_call_target="Cholesky" | custom-call | tf_op jit(solution)/shard_map/jit(cholesky)/cholesky | solution.py:70
  669.1 9.8 %custom-call.60 = f32[1,128,128]{1,2,0:T(8,128)S(1)} custom-call(f32[1,128,128]{2,1,0:T(8,128)S(1)} %get-tuple-element.27), custom_call_target="InvertDiagBlocksLowerTriangular" | custom-call | tf_op jit(solution)/shard_map/jit(cholesky)/cholesky | solution.py:70
  682.3 11.7 %cholesky.468 = f32[128,128]{1,0:T(8,128)S(1)} custom-call(f32[128,128]{1,0:T(8,128)S(1)} %cholesky.589), custom_call_target="Cholesky" | custom-call | tf_op jit(solution)/shard_map/jit(cholesky)/cholesky | solution.py:70
  695.2 9.8 %custom-call.61 = f32[1,128,128]{1,2,0:T(8,128)S(1)} custom-call(f32[1,128,128]{2,1,0:T(8,128)S(1)} %get-tuple-element.24), custom_call_target="InvertDiagBlocksLowerTriangular" | custom-call | tf_op jit(solution)/shard_map/jit(cholesky)/cholesky | solution.py:70
  708.6 11.9 %cholesky.487 = f32[128,128]{1,0:T(8,128)S(1)} custom-call(f32[128,128]{1,0:T(8,128)S(1)} %cholesky.594), custom_call_target="Cholesky" | custom-call | tf_op jit(solution)/shard_map/jit(cholesky)/cholesky | solution.py:70
  721.8 9.8 %custom-call.62 = f32[1,128,128]{1,2,0:T(8,128)S(1)} custom-call(f32[1,128,128]{2,1,0:T(8,128)S(1)} %get-tuple-element.21), custom_call_target="InvertDiagBlocksLowerTriangular" | custom-call | tf_op jit(solution)/shard_map/jit(cholesky)/cholesky | solution.py:70
  735.0 11.7 %cholesky.506 = f32[128,128]{1,0:T(8,128)S(1)} custom-call(f32[128,128]{1,0:T(8,128)S(1)} %cholesky.599), custom_call_target="Cholesky" | custom-call | tf_op jit(solution)/shard_map/jit(cholesky)/cholesky | solution.py:70
  748.0 10.2 %custom-call.63 = f32[1,128,128]{1,2,0:T(8,128)S(1)} custom-call(f32[1,128,128]{2,1,0:T(8,128)S(1)} %get-tuple-element.18), custom_call_target="InvertDiagBlocksLowerTriangular" | custom-call | tf_op jit(solution)/shard_map/jit(cholesky)/cholesky | solution.py:70
  761.6 11.7 %cholesky.526 = f32[128,128]{1,0:T(8,128)S(1)} custom-call(f32[128,128]{1,0:T(8,128)S(1)} %cholesky.604), custom_call_target="Cholesky" | custom-call | tf_op jit(solution)/shard_map/jit(cholesky)/cholesky | solution.py:70
  774.6 9.8 %custom-call.64 = f32[1,128,128]{1,2,0:T(8,128)S(1)} custom-call(f32[1,128,128]{2,1,0:T(8,128)S(1)} %get-tuple-element.15), custom_call_target="InvertDiagBlocksLowerTriangular" | custom-call | tf_op jit(solution)/shard_map/jit(cholesky)/cholesky | solution.py:70
  787.4 11.9 %cholesky.546 = f32[128,128]{1,0:T(8,128)S(1)} custom-call(f32[128,128]{1,0:T(8,128)S(1)} %cholesky.609), custom_call_target="Cholesky" | custom-call | tf_op jit(solution)/shard_map/jit(cholesky)/cholesky | solution.py:70
  800.5 9.8 %custom-call.65 = f32[1,128,128]{1,2,0:T(8,128)S(1)} custom-call(f32[1,128,128]{2,1,0:T(8,128)S(1)} %get-tuple-element.12), custom_call_target="InvertDiagBlocksLowerTriangular" | custom-call | tf_op jit(solution)/shard_map/jit(cholesky)/cholesky | solution.py:70
  812.9 11.7 %cholesky.564 = f32[128,128]{1,0:T(8,128)S(1)} custom-call(f32[128,128]{1,0:T(8,128)S(1)} %convolution_subtract_fusion.6), custom_call_target="Cholesky" | custom-call | tf_op jit(solution)/shard_map/jit(cholesky)/cholesky | solution.py:70
  (72 shorter events, 83.7 us)
Async XLA Ops:
  206.6 9.7 %copy-start.2 = (s32[8192]{0:T(1024)S(1)}, s32[8192]{0:T(1024)}, u32[]{:S(2)}) copy-start(s32[8192]{0:T(1024)} %param.5) | copy-start | bytes 98308
  209.2 56.7 %all-to-all-start.3 = ((f32[64,8,1024]{2,1,0:T(8,128)}), f32[64,8,1024]{2,1,0:T(8,128)S(1)}, u32[]{:S(2)}, u32[]{:S(2)}) async-start(f32[64,8,1024]{2,1,0:T(8,128)} %copy.23), calls=%async_computation.3 | async-start | bytes 4194304 | tf_op jit(solution)/shard_map/all_to_all | solution.py:29
  216.2 262.1 %all-reduce.5.cloned.1.call-start = ((), (), s32[]{:S(2)}) async-start(), calls=%async_computation.5 | async-start | bytes 1048576
  287.6 312.7 %all-gather.3.cloned.1.call-start = ((), (), s32[]{:S(2)}) async-start(), calls=%async_computation.4 | async-start | bytes 4202496 | tf_op jit(solution)/shard_map/all_gather | solution.py:64
  604.4 3.3 copy-start
  618.1 1.9 copy-start.1
Sparse Core Ops, SparseCore 0:
  287.8 190.5 all-reduce.4
  482.5 117.7 all-gather.2
where the time goes:
time: 850 us; the launch traced here: 840 us
  waiting for transfers between devices  356 us (42%)
  blocking collectives  194 us (23%)
  other arithmetic  189 us (22%)
  local copies, waits for them, and re-layouts  37.2 us (4%)
  matrix products  34.8 us (4%)
  between operations  21.3 us (3%)
    unnamed x3, waiting for transfers between devices  189 us
    another operation x30, other arithmetic, local(): lower_factor = jnp.linalg.cholesky(gram_matrix)  181 us
    all_gather x1, waiting for transfers between devices, local(): lax.all_gather(gram_block[None], ('row', 'grp'), axis=0, tiled=True)  121 us
    all_to_all x1, blocking collectives, local(): lax.all_to_all(grp_mixed, 'row', split_axis=1, concat_axis=0, tiled=True)  67.5 us
    all_to_all x1, blocking collectives, local(): lax.all_to_all(local_mix[None], 'grp', split_axis=2, concat_axis=0, tiled...  55.9 us
    all_to_all x1, blocking collectives, mix_grp(): lax.all_to_all(mix_lead(exchanged), 'grp', split_axis=0, concat_axis=2, t...  51.2 us
    all_to_all x1, waiting for transfers between devices, mix_row(): lax.all_to_all(mix_lead(exchanged), 'row', split_axis=0, concat_axis=1, t...  46.9 us
    another operation x14, matrix products, local(): lower_factor = jnp.linalg.cholesky(gram_matrix)  23.1 us
  transfers between devices with their start and end apart: 3, of which 3 were waited for; matrix products, arithmetic and copies ran while one was open for 0% of the time, Pallas kernels for 0%

commit v1 on v0

v1 whole, which is shorter than its diff:
```python
import math

import jax
import jax.numpy as jnp
from jax import lax
from jax.experimental import pallas as pl
from jax.experimental.pallas import tpu as pltpu
from jax.sharding import PartitionSpec as P

HIGHEST = lax.Precision.HIGHEST
MESH = pl.DeviceIdType.MESH
BLOCK = 128
VMEM_LIMIT = 48 * 2**20


def hadamard(table_size, dtype):
    row_ids = lax.broadcasted_iota(jnp.int32, (table_size, table_size), 0)
    col_ids = lax.broadcasted_iota(jnp.int32, (table_size, table_size), 1)
    shared = row_ids & col_ids
    parity = jnp.zeros((table_size, table_size), jnp.int32)
    for bit_pos in range(table_size.bit_length() - 1):
        parity = parity ^ shared >> bit_pos & 1
    return (1 - 2 * parity).astype(dtype)


PARTS = ((0, 640, "xyz"), (640, 256, "yxz"), (896, 256, "zxy"))
SIZES = {"x": 4, "y": 8, "z": 8}


def place():
    row, grp = lax.axis_index("row"), lax.axis_index("grp")
    return {"core": row % 2, "x": row // 2 % 4, "z": row // 8, "y": grp}


def device(where, **other):
    at = dict(where, **other)
    return ((at["z"] * 4 + at["x"]) * 2 + at["core"], at["y"])


def sum_kernel(t_ref, o_ref, c_recv, acc, *rest):
    slots, (send_sem, recv_sem) = rest[:-2], rest[-2:]
    me = place()
    half = t_ref.shape[0] // 2
    barrier = pltpu.get_barrier_semaphore()
    peers = [device(me, core=1 - me["core"])]
    for axis, size in SIZES.items():
        peers += [device(me, **{axis: (me[axis] + off) % size}) for off in range(1, size)]
    for peer in peers:
        pl.semaphore_signal(barrier, inc=1, device_id=peer, device_id_type=MESH)
    pl.semaphore_wait(barrier, len(peers))

    def copy(src, dst, part, stage, off, peer):
        return pltpu.make_async_remote_copy(
            src_ref=src, dst_ref=dst, send_sem=send_sem.at[part, stage, off],
            recv_sem=recv_sem.at[part, stage, off], device_id=peer, device_id_type=MESH)

    def offset(value):
        return pl.multiple_of(value, 8)

    own = offset(me["core"] * half)
    other = offset((1 - me["core"]) * half)
    partner = device(me, core=1 - me["core"])
    flying = {}
    for part, (lo, width, _) in enumerate(PARTS):
        cols = pl.ds(lo, width)
        flying[part] = [copy(t_ref.at[pl.ds(other, half), cols], c_recv.at[:, cols], part, 0, 0, partner)]
        flying[part][0].start()
    started = list(flying.values())

    def peers_of(axis):
        size = SIZES[axis]
        return [(off, (me[axis] + off) % size) for off in range(1, size)]

    state = {}
    for part, (lo, width, order) in enumerate(PARTS):
        cols = pl.ds(lo, width)
        flying[part][0].wait()
        acc[:, cols] = t_ref[pl.ds(own, half), cols] + c_recv[:, cols]
        m = half // SIZES[order[0]]
        flying[part] = [
            copy(acc.at[pl.ds(offset(there * m), m), cols], slots[3 * part].at[off - 1], part, 1, off - 1,
                 device(me, **{order[0]: there}))
            for off, there in peers_of(order[0])]
        for c in flying[part]:
            c.start()
    for part, (lo, width, order) in enumerate(PARTS):
        cols = pl.ds(lo, width)
        m = half // SIZES[order[0]]
        m2 = m // SIZES[order[1]]
        base = offset(me[order[0]] * m)
        for c in flying[part]:
            c.wait()
        total = acc[pl.ds(base, m), cols]
        for k in range(SIZES[order[0]] - 1):
            total = total + slots[3 * part][k]
        acc[pl.ds(base, m), cols] = total
        flying[part] = [
            copy(acc.at[pl.ds(offset(base + there * m2), m2), cols], slots[3 * part + 1].at[off - 1], part, 2, off - 1,
                 device(me, **{order[1]: there}))
            for off, there in peers_of(order[1])]
        for c in flying[part]:
            c.start()
    for part, (lo, width, order) in enumerate(PARTS):
        cols = pl.ds(lo, width)
        m = half // SIZES[order[0]]
        m2 = m // SIZES[order[1]]
        base = offset(me[order[0]] * m + me[order[1]] * m2)
        for c in flying[part]:
            c.wait()
        total = acc[pl.ds(base, m2), cols]
        for k in range(SIZES[order[1]] - 1):
            total = total + slots[3 * part + 1][k]
        acc[pl.ds(base, m2), cols] = total
        flying[part] = [
            copy(acc.at[pl.ds(base, m2), cols], slots[3 * part + 2].at[off - 1], part, 3, off - 1,
                 device(me, **{order[2]: there}))
            for off, there in peers_of(order[2])]
        for c in flying[part]:
            c.start()
    for part, (lo, width, order) in enumerate(PARTS):
        cols = pl.ds(lo, width)
        m = half // SIZES[order[0]]
        m2 = m // SIZES[order[1]]
        base = offset(me[order[0]] * m + me[order[1]] * m2)
        for c in flying[part]:
            c.wait()
        total = acc[pl.ds(base, m2), cols]
        for k in range(SIZES[order[2]] - 1):
            total = total + slots[3 * part + 2][k]
        at = offset(own + base)
        o_ref[pl.ds(at, m2), cols] = total
        piece = o_ref.at[pl.ds(at, m2), cols]
        flying[part] = [
            copy(piece, piece, part, 4, off - 1, device(me, **{order[1]: there}))
            for off, there in peers_of(order[1])]
        for c in flying[part]:
            c.start()
    for part, (lo, width, order) in enumerate(PARTS):
        cols = pl.ds(lo, width)
        m = half // SIZES[order[0]]
        for c in flying[part]:
            c.wait()
        piece = o_ref.at[pl.ds(offset(own + me[order[0]] * m), m), cols]
        flying[part] = [
            copy(piece, piece, part, 5, off - 1, device(me, **{order[0]: there}))
            for off, there in peers_of(order[0])]
        for c in flying[part]:
            c.start()
    for part, (lo, width, order) in enumerate(PARTS):
        cols = pl.ds(lo, width)
        for c in flying[part]:
            c.wait()
        piece = o_ref.at[pl.ds(own, half), cols]
        flying[part] = [copy(piece, piece, part, 6, 0, partner)]
        flying[part][0].start()
    for part in range(len(PARTS)):
        flying[part][0].wait()


def sum_packed(packed):
    rows, width = packed.shape
    half = rows // 2
    slots = []
    for _, cols, order in PARTS:
        m = half // SIZES[order[0]]
        m2 = m // SIZES[order[1]]
        slots += [pltpu.VMEM((SIZES[order[0]] - 1, m, cols), jnp.float32),
                  pltpu.VMEM((SIZES[order[1]] - 1, m2, cols), jnp.float32),
                  pltpu.VMEM((SIZES[order[2]] - 1, m2, cols), jnp.float32)]
    return pl.pallas_call(
        sum_kernel,
        out_shape=jax.ShapeDtypeStruct(packed.shape, jnp.float32),
        in_specs=[pl.BlockSpec(memory_space=pltpu.VMEM)],
        out_specs=pl.BlockSpec(memory_space=pltpu.VMEM),
        scratch_shapes=[pltpu.VMEM((half, width), jnp.float32), pltpu.VMEM((half, width), jnp.float32), *slots,
                        pltpu.SemaphoreType.DMA((len(PARTS), 7, 7)), pltpu.SemaphoreType.DMA((len(PARTS), 7, 7))],
        compiler_params=pltpu.CompilerParams(collective_id=0, has_side_effects=True, vmem_limit_bytes=VMEM_LIMIT),
        name="gram_sum",
    )(packed)


def gram_kernel(w_ref, keep_ref, t_ref):
    size, n_cols = w_ref.shape
    table = hadamard(size, jnp.bfloat16)
    rest = w_ref[...]
    mixed = jnp.zeros_like(rest)
    for _ in range(3):
        head = rest.astype(jnp.bfloat16)
        mixed = mixed + jnp.dot(table, head, preferred_element_type=jnp.float32)
        rest = rest - head.astype(jnp.float32)
    sketch = (mixed * keep_ref[...]).astype(jnp.bfloat16)
    nb = n_cols // BLOCK
    dims = (((0,), (0,)), ((), ()))
    for j in range(nb):
        at = j * BLOCK
        prod = lax.dot_general(sketch[:, at:at + BLOCK], sketch[:, at:], dims, preferred_element_type=jnp.float32)
        fold = min(j, nb - 1 - j)
        start = 0 if j < nb // 2 else n_cols + BLOCK - (nb - j) * BLOCK
        t_ref[fold * BLOCK:(fold + 1) * BLOCK, start:start + (nb - j) * BLOCK] = prod


def partial_gram(w, keep):
    n_cols = w.shape[1]
    return pl.pallas_call(
        gram_kernel,
        out_shape=jax.ShapeDtypeStruct((n_cols // 2, n_cols + BLOCK), jnp.float32),
        in_specs=[pl.BlockSpec(memory_space=pltpu.VMEM)] * 2,
        out_specs=pl.BlockSpec(memory_space=pltpu.VMEM),
        compiler_params=pltpu.CompilerParams(vmem_limit_bytes=VMEM_LIMIT),
        name="gram_part",
    )(w, keep)


def lane(x, l):
    return jnp.broadcast_to(x[:, l:l + 1], (8, BLOCK))


def invert_factor(rows):
    groups = len(rows)
    lanes = lax.broadcasted_iota(jnp.int32, (8, BLOCK), 1)
    subs = lax.broadcasted_iota(jnp.int32, (8, BLOCK), 0)
    rows = list(rows)
    for b in range(groups):
        j0 = 8 * b
        here = rows[b]
        row = [jnp.broadcast_to(here[k:k + 1, :], (8, BLOCK)) for k in range(8)]
        s = {(k, l): lane(row[k], j0 + l) for k in range(8) for l in range(k, 8)}
        below = range(b + 1, groups)
        col = {(q, l): lane(rows[q], j0 + l) for q in below for l in range(8)}
        inside = (lanes >= j0) & (lanes < j0 + 8)
        row = [jnp.where(inside, (lanes == j0 + k).astype(jnp.float32), row[k]) for k in range(8)]
        mult = {}
        root = []
        for k in range(8):
            inv = 1.0 / s[k, k]
            root.append(lax.rsqrt(s[k, k]))
            for i in range(k + 1, 8):
                m = s[k, i] * inv
                for l in range(i, 8):
                    s[i, l] = s[i, l] - m * s[k, l]
                row[i] = row[i] - m * row[k]
            for q in below:
                m = col[q, k] * inv
                mult[q, k] = m
                for l in range(k + 1, 8):
                    col[q, l] = col[q, l] - m * s[k, l]
        for q in below:
            acc = jnp.where(inside, 0.0, rows[q])
            for k in range(8):
                acc = acc - mult[q, k] * row[k]
            rows[q] = acc
        out = row[0] * root[0]
        for k in range(1, 8):
            out = jnp.where(subs == k, row[k] * root[k], out)
        rows[b] = jnp.where(lanes <= subs + j0, out, 0.0)
    return rows


def cholesky_kernel(t_ref, o_ref, a):
    nb = a.shape[0] // BLOCK
    n_cols = nb * BLOCK
    me = place()
    my_row, my_grp = (me["z"] * 4 + me["x"]) * 2 + me["core"], me["y"]
    for j in range(nb):
        fold = min(j, nb - 1 - j)
        start = 0 if j < nb // 2 else n_cols + BLOCK - (nb - j) * BLOCK
        a[j * BLOCK:(j + 1) * BLOCK, j * BLOCK:] = t_ref[
            fold * BLOCK:(fold + 1) * BLOCK, start:start + (nb - j) * BLOCK]
    out_rows = o_ref.shape[0]
    o_ref[...] = jnp.zeros_like(o_ref)

    @pl.loop(0, nb)
    def _(j):
        base = pl.multiple_of(j * BLOCK, BLOCK)
        rows = [a[pl.ds(base + 8 * q, 8), pl.ds(base, BLOCK)] for q in range(BLOCK // 8)]
        inverse = jnp.concatenate(invert_factor(rows), axis=0)
        for t in range(nb):
            @pl.when(j == t)
            def _():
                lo = BLOCK * t
                upper = jnp.dot(inverse, a[lo:lo + BLOCK, lo:], precision=HIGHEST, preferred_element_type=jnp.float32)
                lower = upper.T
                a[lo:, lo:lo + BLOCK] = lower

                @pl.when((my_grp == t) & (my_row * out_rows >= lo))
                def _():
                    first = pl.multiple_of(my_row * out_rows, 8)
                    mine = a[pl.ds(first, out_rows), lo:lo + BLOCK]
                    r = lax.broadcasted_iota(jnp.int32, mine.shape, 0) + first
                    c = lax.broadcasted_iota(jnp.int32, mine.shape, 1) + lo
                    o_ref[...] = jnp.where(r >= c, mine, 0.0)

                for i in range(t + 1, nb):
                    at = BLOCK * i
                    a[at:at + BLOCK, at:] = a[at:at + BLOCK, at:] - jnp.dot(
                        lower[at - lo:at - lo + BLOCK], upper[:, at - lo:],
                        precision=HIGHEST, preferred_element_type=jnp.float32)


def cholesky_share(packed, n_cols, share):
    return pl.pallas_call(
        cholesky_kernel,
        out_shape=jax.ShapeDtypeStruct(share, jnp.float32),
        in_specs=[pl.BlockSpec(memory_space=pltpu.VMEM)],
        out_specs=pl.BlockSpec(memory_space=pltpu.VMEM),
        scratch_shapes=[pltpu.VMEM((n_cols, n_cols), jnp.float32)],
        compiler_params=pltpu.CompilerParams(vmem_limit_bytes=VMEM_LIMIT),
        name="cholesky",
    )(packed)


def local(panel_rows, sign_bits, sample_rows):
    rows_dev, n_cols = panel_rows.shape
    n_row = lax.axis_size("row")
    n_grp = lax.axis_size("grp")
    n_dev = n_row * n_grp
    flipped = panel_rows * (1 - 2 * sign_bits).astype(jnp.bfloat16)[:, None]
    local_mix = jnp.dot(hadamard(rows_dev, jnp.bfloat16), flipped, preferred_element_type=jnp.float32)
    mine = lax.all_to_all(local_mix, ("row", "grp"), 0, 0, tiled=True)
    norm_scale = 1.0 / math.sqrt(rows_dev * n_dev * sample_rows.shape[0])
    position = lax.axis_index("row") * n_grp + lax.axis_index("grp")
    ids = jnp.arange(n_dev, dtype=jnp.int32) * rows_dev + position
    sampled = jnp.any(sample_rows[None, :] == ids[:, None], axis=1)
    keep = jnp.where(sampled, norm_scale, 0.0).astype(jnp.float32)[:, None]
    packed = sum_packed(partial_gram(mine, keep))
    return cholesky_share(packed, n_cols, (n_cols // n_row, n_cols // n_grp))


def solution(mesh):
    return jax.shard_map(
        local,
        mesh=mesh,
        in_specs=(P(("row", "grp"), None), P(("row", "grp")), P()),
        out_specs=P("row", "grp"),
        check_vma=False,
    )
```

time: 850 us -> 177 us (0.21); the launches traced: 840 us -> 176 us
  waiting for transfers between devices: 356 us -> 51.4 us
  blocking collectives: 194 us -> 0 us
  other arithmetic: 189 us -> 2.97 us
  Pallas kernels: 0 us -> 92.9 us
  local copies, waits for them, and re-layouts: 37.2 us -> 4.13 us
  matrix products: 34.8 us -> 2.81 us
  between operations: 21.3 us -> 0.06 us
  starting transfers between devices: 7.1 us -> 22.2 us
    unnamed x3 -> x0, waiting for transfers between devices: 189 us -> none
    another operation x30 -> x0, other arithmetic: 181 us -> none  [local(): lower_factor = jnp.linalg.cholesky(gram_matrix)]
    all_to_all x3 -> x0, blocking collectives: 175 us -> none  [the longest x1 67.5 us: local(): lax.all_to_all(grp_mixed, 'row', split_axis=1, concat_axis=0, tiled=True)]
    all_gather x1 -> x0, waiting for transfers between devices: 121 us -> none  [local(): lax.all_gather(gram_block[None], ('row', 'grp'), axis=0, tiled=True)]
    pallas_call x0 -> x3, Pallas kernels: none -> 92.9 us  [the longest x1 47.7 us: sum_packed(): pl.pallas_call(sum_kernel, out_shape=jax.ShapeDtypeStruct(packed.shape, j...]
    another operation x14 -> x0, matrix products: 23.1 us -> none  [local(): lower_factor = jnp.linalg.cholesky(gram_matrix)]
    all_gather x1 -> x0, blocking collectives: 19.9 us -> none  [local(): shard_rows = lax.all_gather(sketch, 'grp', axis=0, tiled=True)]
    all_to_all x1, starting transfers between devices: 7.02 us -> 22.2 us  [local(): mine = lax.all_to_all(local_mix, ('row', 'grp'), 0, 0, tiled=True)]
  transfers between devices with their start and end apart: 3 -> 1, of which waited for: 3 -> 1; matrix products, arithmetic and copies ran while one was open for 0% -> 1% of each run, Pallas kernels for 0% -> 0%
where the time goes in v1:
time: 177 us; the launch traced here: 176 us
  Pallas kernels  92.9 us (52%)
  waiting for transfers between devices  51.4 us (29%)
  starting transfers between devices  22.2 us (13%)
  local copies, waits for them, and re-layouts  4.13 us (2%)
  other arithmetic  2.97 us (2%)
  matrix products  2.81 us (2%)
    all_to_all x1, waiting for transfers between devices, local(): mine = lax.all_to_all(local_mix, ('row', 'grp'), 0, 0, tiled=True)  51.4 us
    pallas_call x1, Pallas kernels, sum_packed(): pl.pallas_call(sum_kernel, out_shape=jax.ShapeDtypeStruct(packed.shape, j...  47.7 us
    pallas_call x1, Pallas kernels, cholesky_share(): pl.pallas_call(cholesky_kernel, out_shape=jax.ShapeDtypeStruct(share, jnp...  41.8 us
    all_to_all x1, starting transfers between devices, local(): mine = lax.all_to_all(local_mix, ('row', 'grp'), 0, 0, tiled=True)  22.2 us
  transfers between devices with their start and end apart: 1, of which 1 were waited for; matrix products, arithmetic and copies ran while one was open for 1% of the time, Pallas kernels for 0%

profile of v1, /device:TPU:1, one launch (start us, length us, event | category | flops | bytes accessed | tf_op | source)
XLA Modules:
  0.0 176.5 jit_solution(87891435209016229)
XLA Ops:
  0.0 0.7 subtract_convert_fusion.2
  0.7 2.8 %convolution_bitcast_fusion = f32[512,1,1024]{2,0,1:T(8,128)S(1)} fusion(bf16[512,1024]{1,0:T(8,128)(2,1)} %param.3, bf16[512]{0:T(512)(128)(2,1)S(1)} %subtract_convert_fusion.2), kind=kOutput, calls=%fused_computation.2 | convolution fusion | flops 545259520 | bytes 3146752 | tf_op jit(solution)/shard_map/dot_general | solution.py:318
  3.5 3.5 %copy.7 = f32[512,1,1024]{2,1,0:T(1,128)} copy(f32[512,1,1024]{2,0,1:T(8,128)S(1)} %convolution_bitcast_fusion) | data formatting | bytes 4194304 | tf_op jit(solution)/shard_map/all_to_all | solution.py:319
  7.0 0.0 copy-start
  7.0 22.2 %all-to-all-start = ((f32[512,1,1024]{2,1,0:T(1,128)}), f32[512,1,1024]{2,1,0:T(1,128)S(1)}, u32[]{:S(2)}, u32[]{:S(2)}) async-start(f32[512,1,1024]{2,1,0:T(1,128)} %copy.7), calls=%async_computation | async-start | bytes 4194304 | tf_op jit(solution)/shard_map/all_to_all | solution.py:319
  29.2 0.0 copy-done
  29.2 2.3 %compare_reduce_fusion = pred[512]{0:T(512)(128)(4,1)S(1)} fusion(s32[8192]{0:T(1024)S(1)} %copy-done, s32[512]{0:T(512)S(1)} %multiply_add_fusion), kind=kLoop, calls=%fused_computation | loop fusion | flops 8388096 | bytes 35328 | tf_op jit(solution)/shard_map/reduce_or | solution.py:323
  31.5 0.2 copy.8.keep_ref
  31.7 51.4 %all-to-all-done = f32[512,1,1024]{2,1,0:T(1,128)S(1)} async-done(((f32[512,1,1024]{2,1,0:T(1,128)}), f32[512,1,1024]{2,1,0:T(1,128)S(1)}, u32[]{:S(2)}, u32[]{:S(2)}) %all-to-all-start) | async-done | bytes 2097184 | tf_op jit(solution)/shard_map/all_to_all | solution.py:319
  83.1 0.5 copy.11
  83.5 3.5 %gram_part.1.t_ref = f32[512,1152]{1,0:T(8,128)S(1)} custom-call(f32[512,1024]{1,0:T(8,128)S(1)} %bitcast.6, f32[512,1]{1,0:T(8,128)S(1)} %copy.8.keep_ref), custom_call_target="tpu_custom_call" | custom-call | tf_op jit(solution)/shard_map/gram_part/pallas_call | solution.py:204
  87.0 47.7 %gram_sum.1.t_ref = f32[512,1152]{1,0:T(8,128)S(1)} custom-call(f32[512,1152]{1,0:T(8,128)S(1)} %gram_part.1.t_ref), custom_call_target="tpu_custom_call" | custom-call | tf_op jit(solution)/shard_map/gram_sum/pallas_call | solution.py:170
  134.7 41.8 %cholesky.1 = f32[16,128]{1,0:T(8,128)} custom-call(f32[512,1152]{1,0:T(8,128)S(1)} %gram_sum.1.t_ref), custom_call_target="tpu_custom_call" | custom-call | tf_op jit(solution)/shard_map/cholesky/pallas_call | solution.py:301
  (2 shorter events, 0.0 us)
Async XLA Ops:
  7.0 22.2 %copy-start = (s32[8192]{0:T(1024)S(1)}, s32[8192]{0:T(1024)}, u32[]{:S(2)}) copy-start(s32[8192]{0:T(1024)} %param.5) | copy-start | bytes 98308
  7.0 76.1 %all-to-all-start = ((f32[512,1,1024]{2,1,0:T(1,128)}), f32[512,1,1024]{2,1,0:T(1,128)S(1)}, u32[]{:S(2)}, u32[]{:S(2)}) async-start(f32[512,1,1024]{2,1,0:T(1,128)} %copy.7), calls=%async_computation | async-start | bytes 4194304 | tf_op jit(solution)/shard_map/all_to_all | solution.py:319

commit v2 on v0

v2 whole, which is shorter than its diff:
```python
import math

import jax
import jax.numpy as jnp
from jax import lax
from jax.experimental import pallas as pl
from jax.experimental.pallas import tpu as pltpu
from jax.sharding import PartitionSpec as P

HIGHEST = lax.Precision.HIGHEST
MESH = pl.DeviceIdType.MESH
BLOCK = 128
VMEM_LIMIT = 48 * 2**20


def hadamard(table_size, dtype):
    row_ids = lax.broadcasted_iota(jnp.int32, (table_size, table_size), 0)
    col_ids = lax.broadcasted_iota(jnp.int32, (table_size, table_size), 1)
    shared = row_ids & col_ids
    parity = jnp.zeros((table_size, table_size), jnp.int32)
    for bit_pos in range(table_size.bit_length() - 1):
        parity = parity ^ shared >> bit_pos & 1
    return (1 - 2 * parity).astype(dtype)


SIZES = {"x": 4, "y": 8, "z": 8}
STACKS = 4
N_BLOCKS = 8
UPPER = [(i, k) for i in range(N_BLOCKS) for k in range(i, N_BLOCKS)]
CHUNKS = ((4, "xyz"), (4, "xyz"), (8, "xyz"), (8, "yxz"), (12, "zxy"))
FIRST = [sum(n for n, _ in CHUNKS[:c]) for c in range(len(CHUNKS))]
BEFORE = ("g0 s0 g1 s1 g2 a0 a1 s2 g3 a0 a1 a2 g4 a0 a1 a2 s3 a0 a1 a2 a3 s4 a0 a1 a2 a3 a4 a0 a1 a2 a3 a4 f0")
BESIDE = ("f1 a2 a3 a4", "f2 a3 a4", "a3 a4", "f3 a4", "f4")


def staged(texts):
    reached = [0] * len(CHUNKS)
    out = []
    for text in texts:
        steps = []
        for word in text.split():
            c = int(word[1:])
            steps.append((word[0], c, reached[c]))
            reached[c] += word[0] == "a"
        out.append(steps)
    assert reached == [6] * len(CHUNKS)
    return out


def place():
    row, grp = lax.axis_index("row"), lax.axis_index("grp")
    return {"core": row % 2, "x": row // 2 % 4, "z": row // 8, "y": grp}


def device(where, **other):
    at = dict(where, **other)
    return ((at["z"] * 4 + at["x"]) * 2 + at["core"], at["y"])


def spot(block):
    index = UPPER.index(block)
    chunk = max(c for c in range(len(CHUNKS)) if FIRST[c] <= index)
    stack, col = divmod(index - FIRST[chunk], CHUNKS[chunk][0] // STACKS)
    return chunk, pl.ds(stack * BLOCK, BLOCK), pl.ds(col * BLOCK, BLOCK)


def offset(value):
    return pl.multiple_of(value, 8)


class Sum:
    def __init__(self, chunk, refs, send_sem, recv_sem, me):
        order = CHUNKS[chunk][1]
        self.part, self.near, self.slots, self.full = refs[0], refs[1], refs[2:5], refs[5]
        self.order, self.chunk, self.send_sem, self.recv_sem, self.me = order, chunk, send_sem, recv_sem, me
        self.half = self.part.shape[0] // 2
        self.own = offset(me["core"] * self.half)
        self.m1 = self.half // SIZES[order[0]]
        self.m2 = self.m1 // SIZES[order[1]]
        self.base1 = offset(self.own + me[order[0]] * self.m1)
        self.base2 = offset(self.base1 + me[order[1]] * self.m2)

    def copy(self, src, dst, stage, k, peer):
        return pltpu.make_async_remote_copy(
            src_ref=src, dst_ref=dst, send_sem=self.send_sem.at[self.chunk, stage, k],
            recv_sem=self.recv_sem.at[self.chunk, stage, k], device_id=peer, device_id_type=MESH)

    def peers(self, axis):
        size = SIZES[axis]
        there = [(self.me[axis] + off) % size for off in range(1, size)]
        return [(k, t, device(self.me, **{axis: t})) for k, t in enumerate(there)]

    def copies(self, stage):
        part, full, order = self.part, self.full, self.order
        if stage in (0, 6):
            partner = device(self.me, core=1 - self.me["core"])
            if stage == 0:
                other = offset((1 - self.me["core"]) * self.half)
                return [self.copy(part.at[pl.ds(other, self.half)], self.near, stage, 0, partner)]
            piece = full.at[pl.ds(self.own, self.half)]
            return [self.copy(piece, piece, stage, 0, partner)]
        axis = order[{1: 0, 2: 1, 3: 2, 4: 1, 5: 0}[stage]]
        out = []
        for k, t, peer in self.peers(axis):
            if stage == 1:
                src, dst = part.at[pl.ds(offset(self.own + t * self.m1), self.m1)], self.slots[0].at[k]
            elif stage == 2:
                src, dst = part.at[pl.ds(offset(self.base1 + t * self.m2), self.m2)], self.slots[1].at[k]
            elif stage == 3:
                src, dst = part.at[pl.ds(self.base2, self.m2)], self.slots[2].at[k]
            else:
                at, m = (self.base2, self.m2) if stage == 4 else (self.base1, self.m1)
                src = dst = full.at[pl.ds(at, m)]
            out.append(self.copy(src, dst, stage, k, peer))
        return out

    def start(self, stage):
        for c in self.copies(stage):
            c.start()

    def finish(self, stage):
        for c in self.copies(stage):
            c.wait()

    def advance(self, stage):
        self.finish(stage)
        part = self.part
        if stage == 0:
            part[pl.ds(self.own, self.half)] = part[pl.ds(self.own, self.half)] + self.near[...]
        elif stage < 4:
            at, m = (self.base1, self.m1) if stage == 1 else (self.base2, self.m2)
            total = part[pl.ds(at, m)]
            slots = self.slots[stage - 1]
            for k in range(slots.shape[0]):
                total = total + slots[k]
            into = self.full if stage == 3 else part
            into[pl.ds(at, m)] = total
        self.start(stage + 1)


def buffers(blocks, order):
    rows, cols = STACKS * BLOCK, blocks // STACKS * BLOCK
    half = rows // 2
    m1 = half // SIZES[order[0]]
    m2 = m1 // SIZES[order[1]]
    shapes = [(rows, cols), (half, cols), (SIZES[order[0]] - 1, m1, cols), (SIZES[order[1]] - 1, m2, cols),
              (SIZES[order[2]] - 1, m2, cols), (rows, cols)]
    return [pltpu.VMEM(shape, jnp.float32) for shape in shapes]


def lane(x, l):
    return jnp.broadcast_to(x[:, l:l + 1], (8, BLOCK))


def invert_factor(rows, midway):
    groups = len(rows)
    lanes = lax.broadcasted_iota(jnp.int32, (8, BLOCK), 1)
    subs = lax.broadcasted_iota(jnp.int32, (8, BLOCK), 0)
    rows = list(rows)
    for b in range(groups):
        if b == groups // 2:
            midway()
        j0 = 8 * b
        here = rows[b]
        row = [jnp.broadcast_to(here[k:k + 1, :], (8, BLOCK)) for k in range(8)]
        s = {(k, l): lane(row[k], j0 + l) for k in range(8) for l in range(k, 8)}
        below = range(b + 1, groups)
        col = {(q, l): lane(rows[q], j0 + l) for q in below for l in range(8)}
        inside = (lanes >= j0) & (lanes < j0 + 8)
        row = [jnp.where(inside, (lanes == j0 + k).astype(jnp.float32), row[k]) for k in range(8)]
        mult = {}
        root = []
        for k in range(8):
            inv = 1.0 / s[k, k]
            root.append(lax.rsqrt(s[k, k]))
            for i in range(k + 1, 8):
                m = s[k, i] * inv
                for l in range(i, 8):
                    s[i, l] = s[i, l] - m * s[k, l]
                row[i] = row[i] - m * row[k]
            for q in below:
                m = col[q, k] * inv
                mult[q, k] = m
                for l in range(k + 1, 8):
                    col[q, l] = col[q, l] - m * s[k, l]
        for q in below:
            acc = jnp.where(inside, 0.0, rows[q])
            for k in range(8):
                acc = acc - mult[q, k] * row[k]
            rows[q] = acc
        out = row[0] * root[0]
        for k in range(1, 8):
            out = jnp.where(subs == k, row[k] * root[k], out)
        rows[b] = jnp.where(lanes <= subs + j0, out, 0.0)
    return rows


def factor_kernel(w_ref, keep_ref, o_ref, sketch, a, send_sem, recv_sem, *chunk_refs):
    me = place()
    barrier = pltpu.get_barrier_semaphore()
    peers = [device(me, core=1 - me["core"])]
    for axis, size in SIZES.items():
        peers += [device(me, **{axis: (me[axis] + off) % size}) for off in range(1, size)]
    for peer in peers:
        pl.semaphore_signal(barrier, inc=1, device_id=peer, device_id_type=MESH)

    size = w_ref.shape[0]
    table = hadamard(size, jnp.bfloat16)
    rest = w_ref[...]
    mixed = jnp.zeros_like(rest)
    for _ in range(3):
        head = rest.astype(jnp.bfloat16)
        mixed = mixed + jnp.dot(table, head, preferred_element_type=jnp.float32)
        rest = rest - head.astype(jnp.float32)
    sketch[...] = (mixed * keep_ref[...]).astype(jnp.bfloat16)

    per = len(chunk_refs) // len(CHUNKS)
    sums = [Sum(c, chunk_refs[per * c:per * c + per], send_sem, recv_sem, me) for c in range(len(CHUNKS))]

    def gram(c):
        blocks = UPPER[FIRST[c]:FIRST[c] + CHUNKS[c][0]]
        for i in sorted({i for i, _ in blocks}):
            ks = [k for bi, k in blocks if bi == i]
            wide = lax.dot_general(
                sketch[:, i * BLOCK:(i + 1) * BLOCK], sketch[:, ks[0] * BLOCK:(ks[-1] + 1) * BLOCK],
                (((0,), (0,)), ((), ())), preferred_element_type=jnp.float32)
            for n, k in enumerate(ks):
                _, rows, cols = spot((i, k))
                sums[c].part[rows, cols] = wide[:, n * BLOCK:(n + 1) * BLOCK]

    def run(steps):
        for what, c, stage in steps:
            if what == "g":
                gram(c)
                if c == 0:
                    pl.semaphore_wait(barrier, len(peers))
            elif what == "s":
                sums[c].start(stage)
            elif what == "a":
                sums[c].advance(stage)
            else:
                sums[c].finish(stage)

    before, *beside = staged((BEFORE, *BESIDE))
    run(before)

    my_row, my_grp = (me["z"] * SIZES["x"] + me["x"]) * 2 + me["core"], me["y"]
    out_rows = o_ref.shape[0]
    o_ref[...] = jnp.zeros_like(o_ref)

    def place_block(i, k):
        chunk, rows, cols = spot((i, k))
        a[i * BLOCK:(i + 1) * BLOCK, k * BLOCK:(k + 1) * BLOCK] = sums[chunk].full[rows, cols]

    def updated(t, first):
        lo, col = BLOCK * t, BLOCK * first
        a[lo:lo + BLOCK, col:] = a[lo:lo + BLOCK, col:] - jnp.dot(
            a[lo:lo + BLOCK, :lo], a[:lo, col:], precision=HIGHEST, preferred_element_type=jnp.float32)

    place_block(0, 0)

    @pl.loop(0, N_BLOCKS)
    def _(j):
        for t in range(1, N_BLOCKS):
            @pl.when(j == t)
            def _():
                for k in range(t, N_BLOCKS):
                    place_block(t, k)
                updated(t, t)

        base = pl.multiple_of(j * BLOCK, BLOCK)
        rows = [a[pl.ds(base + 8 * q, 8), pl.ds(base, BLOCK)] for q in range(BLOCK // 8)]

        def midway():
            for t, steps in enumerate(beside[0::2]):
                @pl.when(j == t)
                def _():
                    run(steps)

        inverse = jnp.concatenate(invert_factor(rows, midway), axis=0)
        for t in range(N_BLOCKS):
            @pl.when(j == t)
            def _():
                lo = BLOCK * t
                if t == 0:
                    for k in range(1, N_BLOCKS):
                        place_block(0, k)
                upper = jnp.dot(inverse, a[lo:lo + BLOCK, lo:], precision=HIGHEST, preferred_element_type=jnp.float32)
                a[lo:lo + BLOCK, lo:] = upper
                a[lo:, lo:lo + BLOCK] = upper.T

                @pl.when((my_grp == t) & (my_row * out_rows >= lo))
                def _():
                    first = offset(my_row * out_rows)
                    mine = a[pl.ds(first, out_rows), lo:lo + BLOCK]
                    r = lax.broadcasted_iota(jnp.int32, mine.shape, 0) + first
                    c = lax.broadcasted_iota(jnp.int32, mine.shape, 1) + lo
                    o_ref[...] = jnp.where(r >= c, mine, 0.0)

                if 2 * t + 1 < len(beside):
                    run(beside[2 * t + 1])


def factor_share(w, keep, share):
    n_cols = w.shape[1]
    scratch = [pltpu.VMEM(w.shape, jnp.bfloat16), pltpu.VMEM((n_cols, n_cols), jnp.float32)]
    scratch += [pltpu.SemaphoreType.DMA((len(CHUNKS), 7, 7))] * 2
    for blocks, order in CHUNKS:
        scratch += buffers(blocks, order)
    return pl.pallas_call(
        factor_kernel,
        out_shape=jax.ShapeDtypeStruct(share, jnp.float32),
        in_specs=[pl.BlockSpec(memory_space=pltpu.VMEM)] * 2,
        out_specs=pl.BlockSpec(memory_space=pltpu.VMEM),
        scratch_shapes=scratch,
        compiler_params=pltpu.CompilerParams(collective_id=0, has_side_effects=True, vmem_limit_bytes=VMEM_LIMIT),
        name="factor",
    )(w, keep)


def local(panel_rows, sign_bits, sample_rows):
    rows_dev, n_cols = panel_rows.shape
    n_row = lax.axis_size("row")
    n_grp = lax.axis_size("grp")
    n_dev = n_row * n_grp
    flipped = panel_rows * (1 - 2 * sign_bits).astype(jnp.bfloat16)[:, None]
    local_mix = jnp.dot(hadamard(rows_dev, jnp.bfloat16), flipped, preferred_element_type=jnp.float32)
    mine = lax.all_to_all(local_mix, ("row", "grp"), 0, 0, tiled=True)
    norm_scale = 1.0 / math.sqrt(rows_dev * n_dev * sample_rows.shape[0])
    position = lax.axis_index("row") * n_grp + lax.axis_index("grp")
    ids = jnp.arange(n_dev, dtype=jnp.int32) * rows_dev + position
    sampled = jnp.any(sample_rows[None, :] == ids[:, None], axis=1)
    keep = jnp.where(sampled, norm_scale, 0.0).astype(jnp.float32)[:, None]
    return factor_share(mine, keep, (n_cols // n_row, n_cols // n_grp))


def solution(mesh):
    return jax.shard_map(
        local,
        mesh=mesh,
        in_specs=(P(("row", "grp"), None), P(("row", "grp")), P()),
        out_specs=P("row", "grp"),
        check_vma=False,
    )
```

time: 850 us -> 182 us (0.21)
  waiting for transfers between devices: 356 us -> 51.4 us
  blocking collectives: 194 us -> 0 us
  other arithmetic: 189 us -> 2.97 us
  Pallas kernels: 0 us -> 96.1 us
  local copies, waits for them, and re-layouts: 37.2 us -> 4.73 us
  matrix products: 34.8 us -> 2.81 us
  between operations: 21.3 us -> 0.06 us
  starting transfers between devices: 7.1 us -> 22.2 us
    unnamed x3 -> x0, waiting for transfers between devices: 189 us -> none
    another operation x30 -> x0, other arithmetic: 181 us -> none  [local(): lower_factor = jnp.linalg.cholesky(gram_matrix)]
    all_to_all x3 -> x0, blocking collectives: 175 us -> none  [the longest x1 67.5 us: local(): lax.all_to_all(grp_mixed, 'row', split_axis=1, concat_axis=0, tiled=True)]
    all_gather x1 -> x0, waiting for transfers between devices: 121 us -> none  [local(): lax.all_gather(gram_block[None], ('row', 'grp'), axis=0, tiled=True)]
    pallas_call x0 -> x1, Pallas kernels: none -> 96.1 us  [factor_share(): pl.pallas_call(factor_kernel, out_shape=jax.ShapeDtypeStruct(share, jnp.f...]
    another operation x14 -> x0, matrix products: 23.1 us -> none  [local(): lower_factor = jnp.linalg.cholesky(gram_matrix)]
    all_gather x1 -> x0, blocking collectives: 19.9 us -> none  [local(): shard_rows = lax.all_gather(sketch, 'grp', axis=0, tiled=True)]
    all_to_all x1, starting transfers between devices: 7.02 us -> 22.2 us  [local(): mine = lax.all_to_all(local_mix, ('row', 'grp'), 0, 0, tiled=True)]
  transfers between devices with their start and end apart: 3 -> 1, of which waited for: 3 -> 1; matrix products, arithmetic and copies ran while one was open for 0% -> 1% of each run, Pallas kernels for 0% -> 0%
where the time goes in v2:
time: 182 us; the launch traced here: 180 us
  Pallas kernels  96.1 us (53%)
  waiting for transfers between devices  51.4 us (28%)
  starting transfers between devices  22.2 us (12%)
  local copies, waits for them, and re-layouts  4.73 us (3%)
  other arithmetic  2.97 us (2%)
  matrix products  2.81 us (2%)
    pallas_call x1, Pallas kernels, factor_share(): pl.pallas_call(factor_kernel, out_shape=jax.ShapeDtypeStruct(share, jnp.f...  96.1 us
    all_to_all x1, waiting for transfers between devices, local(): mine = lax.all_to_all(local_mix, ('row', 'grp'), 0, 0, tiled=True)  51.4 us
    all_to_all x1, starting transfers between devices, local(): mine = lax.all_to_all(local_mix, ('row', 'grp'), 0, 0, tiled=True)  22.2 us
  transfers between devices with their start and end apart: 1, of which 1 were waited for; matrix products, arithmetic and copies ran while one was open for 1% of the time, Pallas kernels for 0%

profile of v2, /device:TPU:1, one launch (start us, length us, event | category | flops | bytes accessed | tf_op | source)
XLA Modules:
  0.0 180.2 jit_solution(13643602307594515294)
XLA Ops:
  0.0 0.7 subtract_convert_fusion.2
  0.7 2.8 %convolution_bitcast_fusion = f32[512,1,1024]{2,0,1:T(8,128)S(1)} fusion(bf16[512,1024]{1,0:T(8,128)(2,1)} %param.3, bf16[512]{0:T(512)(128)(2,1)S(1)} %subtract_convert_fusion.2), kind=kOutput, calls=%fused_computation.2 | convolution fusion | flops 545259520 | bytes 3146752 | tf_op jit(solution)/shard_map/dot_general | solution.py:327
  3.5 3.5 %copy.7 = f32[512,1,1024]{2,1,0:T(1,128)} copy(f32[512,1,1024]{2,0,1:T(8,128)S(1)} %convolution_bitcast_fusion) | data formatting | bytes 4194304 | tf_op jit(solution)/shard_map/all_to_all | solution.py:328
  7.0 0.0 copy-start
  7.0 22.2 %all-to-all-start = ((f32[512,1,1024]{2,1,0:T(1,128)}), f32[512,1,1024]{2,1,0:T(1,128)S(1)}, u32[]{:S(2)}, u32[]{:S(2)}) async-start(f32[512,1,1024]{2,1,0:T(1,128)} %copy.7), calls=%async_computation | async-start | bytes 4194304 | tf_op jit(solution)/shard_map/all_to_all | solution.py:328
  29.2 0.0 copy-done
  29.2 2.3 %compare_reduce_fusion = pred[512]{0:T(512)(128)(4,1)S(1)} fusion(s32[8192]{0:T(1024)S(1)} %copy-done, s32[512]{0:T(512)S(1)} %multiply_add_fusion), kind=kLoop, calls=%fused_computation | loop fusion | flops 8388096 | bytes 35328 | tf_op jit(solution)/shard_map/reduce_or | solution.py:332
  31.5 0.2 copy.8.keep_ref
  31.7 51.4 %all-to-all-done = f32[512,1,1024]{2,1,0:T(1,128)S(1)} async-done(((f32[512,1,1024]{2,1,0:T(1,128)}), f32[512,1,1024]{2,1,0:T(1,128)S(1)}, u32[]{:S(2)}, u32[]{:S(2)}) %all-to-all-start) | async-done | bytes 2097184 | tf_op jit(solution)/shard_map/all_to_all | solution.py:328
  83.1 0.5 copy.11
  83.5 96.1 %factor.1 = f32[16,128]{1,0:T(8,128)S(1)} custom-call(f32[512,1024]{1,0:T(8,128)S(1)} %bitcast.6, f32[512,1]{1,0:T(8,128)S(1)} %copy.8.keep_ref), custom_call_target="tpu_custom_call" | custom-call | tf_op jit(solution)/shard_map/factor/pallas_call | solution.py:310
  179.6 0.6 copy.13
  (2 shorter events, 0.0 us)
Async XLA Ops:
  7.0 22.2 %copy-start = (s32[8192]{0:T(1024)S(1)}, s32[8192]{0:T(1024)}, u32[]{:S(2)}) copy-start(s32[8192]{0:T(1024)} %param.5) | copy-start | bytes 98308
  7.0 76.1 %all-to-all-start = ((f32[512,1,1024]{2,1,0:T(1,128)}), f32[512,1,1024]{2,1,0:T(1,128)S(1)}, u32[]{:S(2)}, u32[]{:S(2)}) async-start(f32[512,1,1024]{2,1,0:T(1,128)} %copy.7), calls=%async_computation | async-start | bytes 4194304 | tf_op jit(solution)/shard_map/all_to_all | solution.py:328

commit v3 on v2

--- a/solution.py
+++ b/solution.py
@@ -27,10 +27,10 @@
 STACKS = 4
 N_BLOCKS = 8
 UPPER = [(i, k) for i in range(N_BLOCKS) for k in range(i, N_BLOCKS)]
-CHUNKS = ((4, "xyz"), (4, "xyz"), (8, "xyz"), (8, "yxz"), (12, "zxy"))
+CHUNKS = ((20, "xyz"), (8, "yxz"), (8, "zxy"))
 FIRST = [sum(n for n, _ in CHUNKS[:c]) for c in range(len(CHUNKS))]
-BEFORE = ("g0 s0 g1 s1 g2 a0 a1 s2 g3 a0 a1 a2 g4 a0 a1 a2 s3 a0 a1 a2 a3 s4 a0 a1 a2 a3 a4 a0 a1 a2 a3 a4 f0")
-BESIDE = ("f1 a2 a3 a4", "f2 a3 a4", "a3 a4", "f3 a4", "f4")
+BEFORE = ("g0", "s0", "g1", "s1", "g2", "s2", "a0", "a1", "a2", "a0", "a1", "a2", "a0", "a1", "a2", "a0", "a1", "a2", "a0", "a1", "a2", "a0", "a1", "a2", "f0", "f1", "f2")
+BESIDE = ()
 
 
 def staged(texts):
@@ -38,7 +38,7 @@
     out = []
     for text in texts:
         steps = []
-        for word in text.split():
+        for word in text:
             c = int(word[1:])
             steps.append((word[0], c, reached[c]))
             reached[c] += word[0] == "a"
@@ -146,6 +146,10 @@
     shapes = [(rows, cols), (half, cols), (SIZES[order[0]] - 1, m1, cols), (SIZES[order[1]] - 1, m2, cols),
               (SIZES[order[2]] - 1, m2, cols), (rows, cols)]
     return [pltpu.VMEM(shape, jnp.float32) for shape in shapes]
+
+
+def hadamard_list(size):
+    return [[1 - 2 * ((i & k).bit_count() % 2) for k in range(size)] for i in range(size)]
 
 
 def lane(x, l):
@@ -195,24 +199,140 @@
     return rows
 
 
-def factor_kernel(w_ref, keep_ref, o_ref, sketch, a, send_sem, recv_sem, *chunk_refs):
+def factor_kernel(panel_ref, sign_ref, ids_ref, o_ref, table, mixed, mid_y, mid_r, got, keep, sketch, a,
+                  swap_sem, send_sem, recv_sem, *chunk_refs):
     me = place()
+    n_dev = got.shape[0] * got.shape[1]
+    rows_dev, n_cols = panel_ref.shape
+    n_row, n_grp, n_chip = got.shape[0], got.shape[1], got.shape[0] // 2
+    my_row, my_grp, core = (me["z"] * SIZES["x"] + me["x"]) * 2 + me["core"], me["y"], me["core"]
+    my_chip = my_row // 2
+    half = rows_dev // 2
+
     barrier = pltpu.get_barrier_semaphore()
-    peers = [device(me, core=1 - me["core"])]
-    for axis, size in SIZES.items():
-        peers += [device(me, **{axis: (me[axis] + off) % size}) for off in range(1, size)]
-    for peer in peers:
-        pl.semaphore_signal(barrier, inc=1, device_id=peer, device_id_type=MESH)
-
-    size = w_ref.shape[0]
-    table = hadamard(size, jnp.bfloat16)
-    rest = w_ref[...]
-    mixed = jnp.zeros_like(rest)
-    for _ in range(3):
-        head = rest.astype(jnp.bfloat16)
-        mixed = mixed + jnp.dot(table, head, preferred_element_type=jnp.float32)
-        rest = rest - head.astype(jnp.float32)
-    sketch[...] = (mixed * keep_ref[...]).astype(jnp.bfloat16)
+
+    def next_chip(off):
+        return (my_chip + off) % n_chip
+
+    def greet(row, grp):
+        pl.semaphore_signal(barrier, inc=1, device_id=(row, grp), device_id_type=MESH)
+
+    for off in range(1, n_grp):
+        greet(my_row, (my_grp + off) % n_grp)
+    greet(my_row + 1 - 2 * core, my_grp)
+
+    @pl.loop(1, n_chip)
+    def _(off):
+        greet(2 * next_chip(off), my_grp)
+        greet(2 * next_chip(off) + 1, my_grp)
+
+    base = hadamard(BLOCK, jnp.float32)
+    corner = hadamard_list(rows_dev // BLOCK)
+    flip = (1 - 2 * sign_ref[...]).astype(jnp.float32)
+    for i, signs in enumerate(corner):
+        for k, sign in enumerate(signs):
+            table[i * BLOCK:(i + 1) * BLOCK, k * BLOCK:(k + 1) * BLOCK] = (base * sign).astype(jnp.bfloat16)
+    flat = mixed.reshape(rows_dev * 8, BLOCK)
+
+    def mix(h):
+        signed = (table[h * half:(h + 1) * half, :].astype(jnp.float32) * flip).astype(jnp.bfloat16)
+        part = jnp.dot(signed, panel_ref[...], preferred_element_type=jnp.float32)
+        for k in range(8):
+            flat[pl.ds(h * half * 8 + k, half, 8), :] = part[:, k * BLOCK:(k + 1) * BLOCK]
+
+    def remote(src, dst, sem, row, grp):
+        return pltpu.make_async_remote_copy(
+            src_ref=src, dst_ref=dst, send_sem=swap_sem.at[0, sem], recv_sem=swap_sem.at[1, sem],
+            device_id=(row, grp), device_id_type=MESH)
+
+    def here(src, dst, sem):
+        return pltpu.make_async_copy(src, dst, swap_sem.at[0, sem])
+
+    def waits(sent, received, sem):
+        if sent is not None:
+            remote(sent, sent, sem, my_row, my_grp).wait_send()
+        if received is not None:
+            remote(received, received, sem, my_row, my_grp).wait_recv()
+
+    mix(0)
+    pl.semaphore_wait(barrier, n_row + n_grp - 2)
+    per_grp = half // n_grp
+    for off in range(1, n_grp):
+        t = (my_grp + off) % n_grp
+        remote(mixed.at[pl.ds(t * per_grp, per_grp)], mid_y.at[my_grp], off, my_row, t).start()
+    own_y = here(mixed.at[pl.ds(my_grp * per_grp, per_grp)], mid_y.at[my_grp], 8)
+    own_y.start()
+    mix(1)
+
+    def to_second(chip):
+        return remote(mixed.at[pl.ds(half + chip * n_grp, n_grp)], mid_r.at[my_row], 0, 2 * chip + 1, my_grp)
+
+    own_r = here(mixed.at[pl.ds(half + my_chip * n_grp, n_grp)], mid_r.at[my_row], 9)
+
+    @pl.loop(1, n_chip)
+    def _(off):
+        to_second(next_chip(off)).start()
+
+    @pl.when(core == 0)
+    def _():
+        to_second(my_chip).start()
+
+    @pl.when(core == 1)
+    def _():
+        own_r.start()
+
+    position = jnp.where(core == 0, my_grp * n_chip + my_chip, half + my_chip * n_grp + my_grp)
+    wanted = lax.broadcasted_iota(jnp.int32, (n_dev, BLOCK), 0) * rows_dev + position
+    hits = jnp.zeros((n_dev, BLOCK), jnp.int32)
+    for i in range(ids_ref.shape[0]):
+        hits = jnp.where(ids_ref[i:i + 1, :] == wanted, 1, hits)
+    norm_scale = 1.0 / math.sqrt(rows_dev * n_dev * ids_ref.shape[0] * ids_ref.shape[1])
+    keep[...] = jnp.max(hits, axis=1, keepdims=True).astype(jnp.float32) * norm_scale
+
+    for off in range(1, n_grp):
+        remote(mid_y.at[0], mid_y.at[0], off, my_row, my_grp).wait()
+    own_y.wait()
+
+    def to_first(chip):
+        return remote(mid_y.at[:, chip], got.at[my_row], 10, 2 * chip, my_grp)
+
+    own_f = here(mid_y.at[:, my_chip], got.at[my_row], 11)
+
+    @pl.loop(1, n_chip)
+    def _(off):
+        to_first(next_chip(off)).start()
+
+    @pl.when(core == 1)
+    def _():
+        to_first(my_chip).start()
+        own_r.wait()
+        waits(mid_r.at[pl.ds(0, n_chip - 1)], mid_r.at[pl.ds(0, n_row - 1)], 0)
+        for off in range(1, n_grp):
+            t = (my_grp + off) % n_grp
+            remote(mid_r.at[:, t], got.at[:, my_grp], 11 + off, my_row, t).start()
+        own_g = here(mid_r.at[:, my_grp], got.at[:, my_grp], 11)
+        own_g.start()
+        waits(got.at[pl.ds(0, n_chip)], None, 10)
+        for off in range(1, n_grp):
+            remote(got.at[:, 0], got.at[:, 0], 11 + off, my_row, my_grp).wait()
+        own_g.wait()
+
+    @pl.when(core == 0)
+    def _():
+        own_f.start()
+        waits(mid_r.at[pl.ds(0, n_chip)], None, 0)
+        waits(got.at[pl.ds(0, n_chip - 1)], got.at[pl.ds(0, n_row - 1)], 10)
+        own_f.wait()
+
+    flat_got = got.reshape(n_dev * 8, BLOCK)
+    for k in range(0, 8, 2):
+        rest = jnp.concatenate([flat_got[pl.ds(k, n_dev, 8), :], flat_got[pl.ds(k + 1, n_dev, 8), :]], axis=1)
+        total = jnp.zeros_like(rest)
+        for _ in range(3):
+            top = rest.astype(jnp.bfloat16)
+            total = total + jnp.dot(table[...], top, preferred_element_type=jnp.float32)
+            rest = rest - top.astype(jnp.float32)
+        sketch[:, k * BLOCK:(k + 2) * BLOCK] = (total * keep[...]).astype(jnp.bfloat16)
 
     per = len(chunk_refs) // len(CHUNKS)
     sums = [Sum(c, chunk_refs[per * c:per * c + per], send_sem, recv_sem, me) for c in range(len(CHUNKS))]
@@ -232,8 +352,6 @@
         for what, c, stage in steps:
             if what == "g":
                 gram(c)
-                if c == 0:
-                    pl.semaphore_wait(barrier, len(peers))
             elif what == "s":
                 sums[c].start(stage)
             elif what == "a":
@@ -244,7 +362,6 @@
     before, *beside = staged((BEFORE, *BESIDE))
     run(before)
 
-    my_row, my_grp = (me["z"] * SIZES["x"] + me["x"]) * 2 + me["core"], me["y"]
     out_rows = o_ref.shape[0]
     o_ref[...] = jnp.zeros_like(o_ref)
 
@@ -301,37 +418,37 @@
                     run(beside[2 * t + 1])
 
 
-def factor_share(w, keep, share):
-    n_cols = w.shape[1]
-    scratch = [pltpu.VMEM(w.shape, jnp.bfloat16), pltpu.VMEM((n_cols, n_cols), jnp.float32)]
+def factor_share(panel_rows, signs, ids, n_row, n_grp):
+    rows_dev, n_cols = panel_rows.shape
+    tile = (n_cols // BLOCK, BLOCK)
+    scratch = [
+        pltpu.VMEM((rows_dev, rows_dev), jnp.bfloat16),
+        pltpu.VMEM((rows_dev, *tile), jnp.float32),
+        pltpu.VMEM((n_grp, n_row // 2, *tile), jnp.float32),
+        pltpu.VMEM((n_row, n_grp, *tile), jnp.float32),
+        pltpu.VMEM((n_row, n_grp, *tile), jnp.float32),
+        pltpu.VMEM((n_row * n_grp, 1), jnp.float32),
+        pltpu.VMEM((n_row * n_grp, n_cols), jnp.bfloat16),
+        pltpu.VMEM((n_cols, n_cols), jnp.float32),
+        pltpu.SemaphoreType.DMA((2, 19)),
+    ]
     scratch += [pltpu.SemaphoreType.DMA((len(CHUNKS), 7, 7))] * 2
     for blocks, order in CHUNKS:
         scratch += buffers(blocks, order)
     return pl.pallas_call(
         factor_kernel,
-        out_shape=jax.ShapeDtypeStruct(share, jnp.float32),
-        in_specs=[pl.BlockSpec(memory_space=pltpu.VMEM)] * 2,
+        out_shape=jax.ShapeDtypeStruct((n_cols // n_row, n_cols // n_grp), jnp.float32),
+        in_specs=[pl.BlockSpec(memory_space=pltpu.VMEM)] * 3,
         out_specs=pl.BlockSpec(memory_space=pltpu.VMEM),
         scratch_shapes=scratch,
         compiler_params=pltpu.CompilerParams(collective_id=0, has_side_effects=True, vmem_limit_bytes=VMEM_LIMIT),
         name="factor",
-    )(w, keep)
+    )(panel_rows, signs, ids)
 
 
 def local(panel_rows, sign_bits, sample_rows):
-    rows_dev, n_cols = panel_rows.shape
-    n_row = lax.axis_size("row")
-    n_grp = lax.axis_size("grp")
-    n_dev = n_row * n_grp
-    flipped = panel_rows * (1 - 2 * sign_bits).astype(jnp.bfloat16)[:, None]
-    local_mix = jnp.dot(hadamard(rows_dev, jnp.bfloat16), flipped, preferred_element_type=jnp.float32)
-    mine = lax.all_to_all(local_mix, ("row", "grp"), 0, 0, tiled=True)
-    norm_scale = 1.0 / math.sqrt(rows_dev * n_dev * sample_rows.shape[0])
-    position = lax.axis_index("row") * n_grp + lax.axis_index("grp")
-    ids = jnp.arange(n_dev, dtype=jnp.int32) * rows_dev + position
-    sampled = jnp.any(sample_rows[None, :] == ids[:, None], axis=1)
-    keep = jnp.where(sampled, norm_scale, 0.0).astype(jnp.float32)[:, None]
-    return factor_share(mine, keep, (n_cols // n_row, n_cols // n_grp))
+    return factor_share(panel_rows, sign_bits[None, :], sample_rows.reshape(-1, BLOCK),
+                        lax.axis_size("row"), lax.axis_size("grp"))
 
 
 def solution(mesh):

time: 182 us -> 159 us (0.87)
  Pallas kernels: 96.1 us -> 155 us
  waiting for transfers between devices: 51.4 us -> 0 us
  starting transfers between devices: 22.2 us -> 0 us
  other arithmetic: 2.97 us -> 0 us
  matrix products: 2.81 us -> 0 us
    pallas_call x1, Pallas kernels: 96.1 us -> 155 us  [factor_share(): pl.pallas_call(factor_kernel, out_shape=jax.ShapeDtypeStruct((n_cols // n...]
    all_to_all x1 -> x0, waiting for transfers between devices: 51.4 us -> none  [local(): mine = lax.all_to_all(local_mix, ('row', 'grp'), 0, 0, tiled=True)]
    all_to_all x1 -> x0, starting transfers between devices: 22.2 us -> none  [local(): mine = lax.all_to_all(local_mix, ('row', 'grp'), 0, 0, tiled=True)]
    all_to_all x1 -> x0, local copies, waits for them, and re-layouts: 3.51 us -> none  [local(): mine = lax.all_to_all(local_mix, ('row', 'grp'), 0, 0, tiled=True)]
    dot_general x1 -> x0, matrix products: 2.81 us -> none  [local(): jnp.dot(hadamard(rows_dev, jnp.bfloat16), flipped, preferred_element_type...]
    reduce_or x1 -> x0, other arithmetic: 2.27 us -> none  [local(): sampled = jnp.any(sample_rows[None, :] == ids[:, None], axis=1)]
    unnamed x4 -> x7, local copies, waits for them, and re-layouts: 1.07 us -> 3.26 us
  transfers between devices with their start and end apart: 1 -> 0, of which waited for: 1 -> 0; matrix products, arithmetic and copies ran while one was open for 1% -> 0% of each run, Pallas kernels for 0% -> 0%
where the time goes in v3:
time: 159 us
  Pallas kernels  155 us (97%)
  local copies, waits for them, and re-layouts  3.26 us (2%)
    pallas_call x1, Pallas kernels, factor_share(): pl.pallas_call(factor_kernel, out_shape=jax.ShapeDtypeStruct((n_cols // n...  155 us
    unnamed x7, local copies, waits for them, and re-layouts  3.26 us

profile of v3, /device:TPU:1, one launch (start us, length us, event | category | flops | bytes accessed | tf_op | source)
XLA Modules:
  0.0 158.7 jit_solution(14514335990890346720)
XLA Ops:
  0.0 0.0 copy-start.2
  0.0 0.7 copy-done.2
  0.7 0.0 copy-start
  0.7 1.2 copy-done
  1.9 0.0 copy-start.1
  1.9 0.8 copy-done.1
  2.7 155.4 %factor.1 = f32[16,128]{1,0:T(8,128)S(1)} custom-call(bf16[512,1024]{1,0:T(8,128)(2,1)S(1)} %copy-done, s32[1,512]{1,0:T(1,128)S(1)} %bitcast.3, s32[64,128]{1,0:T(8,128)S(1)} %bitcast.2), custom_call_target="tpu_custom_call" | custom-call | tf_op jit(solution)/shard_map/factor/pallas_call | solution.py:438
  158.1 0.6 copy.5
Async XLA Ops:
  0.0 0.7 copy-start.2
  0.7 1.2 copy-start
  1.9 0.8 copy-start.1

commit v4 on v3

--- a/solution.py
+++ b/solution.py
@@ -27,9 +27,9 @@
 STACKS = 4
 N_BLOCKS = 8
 UPPER = [(i, k) for i in range(N_BLOCKS) for k in range(i, N_BLOCKS)]
-CHUNKS = ((20, "xyz"), (8, "yxz"), (8, "zxy"))
+CHUNKS = ((12, "xyz"), (8, "xzy"), (8, "yxz"), (8, "zxy"))
 FIRST = [sum(n for n, _ in CHUNKS[:c]) for c in range(len(CHUNKS))]
-BEFORE = ("g0", "s0", "g1", "s1", "g2", "s2", "a0", "a1", "a2", "a0", "a1", "a2", "a0", "a1", "a2", "a0", "a1", "a2", "a0", "a1", "a2", "a0", "a1", "a2", "f0", "f1", "f2")
+BEFORE = ("g0", "s0", "g1", "s1", "g2", "s2", "g3", "s3", "a0", "a1", "a2", "a3", "a0", "a1", "a2", "a3", "a0", "a1", "a2", "a3", "a0", "a1", "a2", "a3", "a0", "a1", "a2", "a3", "a0", "a1", "a2", "a3", "f0", "f1", "f2", "f3")
 BESIDE = ()
 
 
@@ -173,17 +173,17 @@
         inside = (lanes >= j0) & (lanes < j0 + 8)
         row = [jnp.where(inside, (lanes == j0 + k).astype(jnp.float32), row[k]) for k in range(8)]
         mult = {}
-        root = []
         for k in range(8):
-            inv = 1.0 / s[k, k]
-            root.append(lax.rsqrt(s[k, k]))
+            root = lax.rsqrt(s[k, k])
+            row[k] = row[k] * root
+            for l in range(k + 1, 8):
+                s[k, l] = s[k, l] * root
             for i in range(k + 1, 8):
-                m = s[k, i] * inv
                 for l in range(i, 8):
-                    s[i, l] = s[i, l] - m * s[k, l]
-                row[i] = row[i] - m * row[k]
+                    s[i, l] = s[i, l] - s[k, i] * s[k, l]
+                row[i] = row[i] - s[k, i] * row[k]
             for q in below:
-                m = col[q, k] * inv
+                m = col[q, k] * root
                 mult[q, k] = m
                 for l in range(k + 1, 8):
                     col[q, l] = col[q, l] - m * s[k, l]
@@ -192,9 +192,9 @@
             for k in range(8):
                 acc = acc - mult[q, k] * row[k]
             rows[q] = acc
-        out = row[0] * root[0]
+        out = row[0]
         for k in range(1, 8):
-            out = jnp.where(subs == k, row[k] * root[k], out)
+            out = jnp.where(subs == k, row[k], out)
         rows[b] = jnp.where(lanes <= subs + j0, out, 0.0)
     return rows
 

time: 159 us -> 155 us (0.975)
  Pallas kernels: 155 us -> 152 us
    pallas_call x1, Pallas kernels: 155 us -> 152 us  [factor_share(): pl.pallas_call(factor_kernel, out_shape=jax.ShapeDtypeStruct((n_cols // n...]
where the time goes in v4:
time: 155 us
  Pallas kernels  152 us (98%)
  local copies, waits for them, and re-layouts  3.26 us (2%)
    pallas_call x1, Pallas kernels, factor_share(): pl.pallas_call(factor_kernel, out_shape=jax.ShapeDtypeStruct((n_cols // n...  152 us
    unnamed x7, local copies, waits for them, and re-layouts  3.26 us

profile of v4, /device:TPU:1, one launch (start us, length us, event | category | flops | bytes accessed | tf_op | source)
XLA Modules:
  0.0 154.9 jit_solution(11626556312294196007)
XLA Ops:
  0.0 0.0 copy-start.2
  0.0 0.7 copy-done.2
  0.7 0.0 copy-start
  0.7 1.2 copy-done
  1.9 0.0 copy-start.1
  1.9 0.8 copy-done.1
  2.7 151.6 %factor.1 = f32[16,128]{1,0:T(8,128)S(1)} custom-call(bf16[512,1024]{1,0:T(8,128)(2,1)S(1)} %copy-done, s32[1,512]{1,0:T(1,128)S(1)} %bitcast.3, s32[64,128]{1,0:T(8,128)S(1)} %bitcast.2), custom_call_target="tpu_custom_call" | custom-call | tf_op jit(solution)/shard_map/factor/pallas_call | solution.py:438
  154.3 0.6 copy.5
Async XLA Ops:
  0.0 0.7 copy-start.2
  0.7 1.2 copy-start
  1.9 0.8 copy-start.1

commit v5 on v4

--- a/solution.py
+++ b/solution.py
@@ -152,6 +152,22 @@
     return [[1 - 2 * ((i & k).bit_count() % 2) for k in range(size)] for i in range(size)]
 
 
+SPAN = 4
+
+
+def dot_split(left, right):
+    def parts(x):
+        high = x.astype(jnp.bfloat16)
+        rest = x - high.astype(jnp.float32)
+        mid = rest.astype(jnp.bfloat16)
+        return high, mid, (rest - mid.astype(jnp.float32)).astype(jnp.bfloat16)
+    h, m, l = parts(left)
+    hh, mm, ll = parts(right)
+    return lax.dot_general(
+        jnp.concatenate([h, h, m, h, l, m], 0), jnp.concatenate([hh, mm, hh, ll, hh, mm], 0),
+        (((0,), (0,)), ((), ())), preferred_element_type=jnp.float32)
+
+
 def lane(x, l):
     return jnp.broadcast_to(x[:, l:l + 1], (8, BLOCK))
 
@@ -165,10 +181,11 @@
         if b == groups // 2:
             midway()
         j0 = 8 * b
+        start = b - b % SPAN
         here = rows[b]
         row = [jnp.broadcast_to(here[k:k + 1, :], (8, BLOCK)) for k in range(8)]
         s = {(k, l): lane(row[k], j0 + l) for k in range(8) for l in range(k, 8)}
-        below = range(b + 1, groups)
+        below = range(b + 1, start + SPAN)
         col = {(q, l): lane(rows[q], j0 + l) for q in below for l in range(8)}
         inside = (lanes >= j0) & (lanes < j0 + 8)
         row = [jnp.where(inside, (lanes == j0 + k).astype(jnp.float32), row[k]) for k in range(8)]
@@ -195,21 +212,36 @@
         out = row[0]
         for k in range(1, 8):
             out = jnp.where(subs == k, row[k], out)
-        rows[b] = jnp.where(lanes <= subs + j0, out, 0.0)
+        rows[b] = out
+        if b + 1 == start + SPAN:
+            low, high = 8 * start, 8 * (b + 1)
+            whole = jnp.concatenate(rows[start:b + 1], axis=0)
+            place_row = lax.broadcasted_iota(jnp.int32, whole.shape, 0) + low
+            place_col = lax.broadcasted_iota(jnp.int32, whole.shape, 1)
+            solved = jnp.where((place_col > place_row) & (place_col < high), 0.0, whole)
+            for q in range(start, b + 1):
+                rows[q] = jnp.where(lanes <= subs + 8 * q, rows[q], 0.0)
+            if b + 1 < groups:
+                taken = dot_split(whole, solved)
+                span_lanes = (lanes >= low) & (lanes < high)
+                for q in range(b + 1, groups):
+                    rows[q] = jnp.where(span_lanes, 0.0, rows[q]) - taken[8 * q:8 * q + 8]
     return rows
 
 
-def factor_kernel(panel_ref, sign_ref, ids_ref, o_ref, table, mixed, mid_y, mid_r, got, keep, sketch, a,
+def factor_kernel(panel_in, sign_ref, ids_ref, o_ref, panel_ref, panel_sem, table, mixed, mid_y, mid_r, got, keep, sketch, a,
                   swap_sem, send_sem, recv_sem, *chunk_refs):
     me = place()
     n_dev = got.shape[0] * got.shape[1]
-    rows_dev, n_cols = panel_ref.shape
+    rows_dev, n_cols = panel_in.shape
     n_row, n_grp, n_chip = got.shape[0], got.shape[1], got.shape[0] // 2
     my_row, my_grp, core = (me["z"] * SIZES["x"] + me["x"]) * 2 + me["core"], me["y"], me["core"]
     my_chip = my_row // 2
     half = rows_dev // 2
 
     barrier = pltpu.get_barrier_semaphore()
+    fetch = pltpu.make_async_copy(panel_in, panel_ref, panel_sem)
+    fetch.start()
 
     def next_chip(off):
         return (my_chip + off) % n_chip
@@ -254,6 +286,7 @@
         if received is not None:
             remote(received, received, sem, my_row, my_grp).wait_recv()
 
+    fetch.wait()
     mix(0)
     pl.semaphore_wait(barrier, n_row + n_grp - 2)
     per_grp = half // n_grp
@@ -422,6 +455,8 @@
     rows_dev, n_cols = panel_rows.shape
     tile = (n_cols // BLOCK, BLOCK)
     scratch = [
+        pltpu.VMEM(panel_rows.shape, panel_rows.dtype),
+        pltpu.SemaphoreType.DMA,
         pltpu.VMEM((rows_dev, rows_dev), jnp.bfloat16),
         pltpu.VMEM((rows_dev, *tile), jnp.float32),
         pltpu.VMEM((n_grp, n_row // 2, *tile), jnp.float32),
@@ -438,7 +473,7 @@
     return pl.pallas_call(
         factor_kernel,
         out_shape=jax.ShapeDtypeStruct((n_cols // n_row, n_cols // n_grp), jnp.float32),
-        in_specs=[pl.BlockSpec(memory_space=pltpu.VMEM)] * 3,
+        in_specs=[pl.BlockSpec(memory_space=pltpu.HBM)] + [pl.BlockSpec(memory_space=pltpu.VMEM)] * 2,
         out_specs=pl.BlockSpec(memory_space=pltpu.VMEM),
         scratch_shapes=scratch,
         compiler_params=pltpu.CompilerParams(collective_id=0, has_side_effects=True, vmem_limit_bytes=VMEM_LIMIT),

time: 155 us -> 155 us (level)
  no operation moved by 1% of the time
where the time goes in v5:
time: 155 us; the launch traced here: 154 us
  Pallas kernels  151 us (97%)
  local copies, waits for them, and re-layouts  3.26 us (2%)
    pallas_call x1, Pallas kernels, factor_share(): pl.pallas_call(factor_kernel, out_shape=jax.ShapeDtypeStruct((n_cols // n...  151 us
    unnamed x7, local copies, waits for them, and re-layouts  3.26 us

profile of v5, /device:TPU:1, one launch (start us, length us, event | category | flops | bytes accessed | tf_op | source)
XLA Modules:
  0.0 154.4 jit_solution(7364066635986631703)
XLA Ops:
  0.0 0.0 copy-start.2
  0.0 0.7 copy-done.2
  0.7 0.0 copy-start
  0.7 1.2 copy-done
  1.9 0.0 copy-start.1
  1.9 0.8 copy-done.1
  2.7 151.1 %factor.1 = f32[16,128]{1,0:T(8,128)S(1)} custom-call(bf16[512,1024]{1,0:T(8,128)(2,1)S(1)} %copy-done, s32[1,512]{1,0:T(1,128)S(1)} %bitcast.3, s32[64,128]{1,0:T(8,128)S(1)} %bitcast.2), custom_call_target="tpu_custom_call" | custom-call | tf_op jit(solution)/shard_map/factor/pallas_call | solution.py:473
  153.8 0.6 copy.5
Async XLA Ops:
  0.0 0.7 copy-start.2
  0.7 1.2 copy-start
  1.9 0.8 copy-start.1
